TPU v7x, 32 devices: a whole 2x2x4 slice. The times are simulated.
32 devices in a mesh: blk: 4 (over y, core), dp: 8 (over z, x).
Axes of the slice: x: 2, y: 2, z: 4, core: 2. Of those that a mesh axis runs over, the one named last changes fastest.
Arguments:
- tokens: bfloat16 [8, 1024, 384], P('dp', 'blk'), may hold values from -6 to 6
- lengths: int32 [8], P('dp'), may hold values from 512 to 1024, as said below
- query_weight: bfloat16 [384, 384], replicated, may hold values from -0.3125 to 0.3125
- query_bias: bfloat16 [384], replicated, may hold values from -1.5 to 1.5
- key_weight: bfloat16 [384, 384], replicated, may hold values from -0.3125 to 0.3125
- key_bias: bfloat16 [384], replicated, may hold values from -1.5 to 1.5
- value_weight: bfloat16 [384, 384], replicated, may hold values from -0.3125 to 0.3125
- value_bias: bfloat16 [384], replicated, may hold values from -1.5 to 1.5
- output_weight: bfloat16 [384, 384], replicated, may hold values from -2.5 to 2.5
- output_bias: bfloat16 [384], replicated, may hold values from -1.5 to 1.5
- first_gain: bfloat16 [384], replicated, may hold values from 0.5 to 1.5
- first_bias: bfloat16 [384], replicated, may hold values from -1.5 to 1.5
- inner_weight: bfloat16 [384, 1536], replicated, may hold values from -0.3125 to 0.3125
- inner_bias: bfloat16 [1536], replicated, may hold values from -1.5 to 1.5
- outer_weight: bfloat16 [1536, 384], replicated, may hold values from -0.15625 to 0.15625
- outer_bias: bfloat16 [384], replicated, may hold values from -1.5 to 1.5
- second_gain: bfloat16 [384], replicated, may hold values from 0.5 to 1.5
- second_bias: bfloat16 [384], replicated, may hold values from -1.5 to 1.5
- relative_table: bfloat16 [512, 384], replicated, may hold values from -6 to 6
- cotangent: bfloat16 [8, 1024, 384], P('dp', 'blk'), may hold values from -18 to 18
Outputs:
- layer_out: float32 [8, 1024, 384], P('dp', 'blk')
- grad_tokens: float32 [8, 1024, 384], P('dp', 'blk')
- grad_query_weight: float32 [384, 384], replicated
- grad_query_bias: float32 [384], replicated
- grad_key_weight: float32 [384, 384], replicated
- grad_key_bias: float32 [384], replicated
- grad_value_weight: float32 [384, 384], replicated
- grad_value_bias: float32 [384], replicated
- grad_output_weight: float32 [384, 384], replicated
- grad_output_bias: float32 [384], replicated
- grad_first_gain: float32 [384], replicated
- grad_first_bias: float32 [384], replicated
- grad_inner_weight: float32 [384, 1536], replicated
- grad_inner_bias: float32 [1536], replicated
- grad_outer_weight: float32 [1536, 384], replicated
- grad_outer_bias: float32 [384], replicated
- grad_second_gain: float32 [384], replicated
- grad_second_bias: float32 [384], replicated
- grad_relative_table: float32 [512, 384], replicated
Inputs may be any that keep to these rules, and one draw needn't show every extreme that they name: `lengths`: one sequence uses all 1024 positions and one uses 1024 // 2.
All inputs are finite; a program needn't handle non-finite values.
Results may differ from a plain program's by a relative error of at most 0.04.
Values may be sent and summed in bfloat16 or wider, within the bound.
No kernel may reach another device: no remote copies, remote signals or barrier semaphores. Data moves between devices by JAX's collectives and lax.ppermute only.
A program may use at most 320 MiB of HBM per device.

v0:
```python
from functools import partial
import math
import jax
import jax.numpy as jnp
from jax import lax
from jax.sharding import PartitionSpec as P

HEADS = 6


def layer_norm(values, gain_vec, bias_vec):
    center = values - jnp.mean(values, axis=-1, keepdims=True)
    spread = jnp.mean(center * center, axis=-1, keepdims=True)
    return center * lax.rsqrt(spread + 1e-07) * gain_vec + bias_vec


def skewed(source_table, row_count, col_count):
    table_width = row_count + col_count - 1
    leading = source_table.shape[:-2]
    padded = jnp.pad(source_table, [(0, 0)] * (source_table.ndim - 1) + [(0, 1)])
    flattened = padded.reshape(leading + (row_count * (table_width + 1),))
    flattened = flattened[..., row_count - 1 : row_count - 1 + row_count * table_width]
    return flattened.reshape(leading + (row_count, table_width))[..., :col_count]


def band_terms(query_table, key_table, band_shift):
    row_count = query_table.shape[2]
    col_count = key_table.shape[2]
    last_index = query_table.shape[3] - 1
    steps_along = jnp.arange(row_count + col_count - 1, dtype=jnp.int32)
    query_index = jnp.clip(band_shift + (row_count - 1) - steps_along, 0, last_index)
    to_position = skewed(jnp.take(query_table, query_index, axis=3), row_count, col_count)
    key_index = jnp.clip(band_shift - (col_count - 1) + steps_along, 0, last_index)
    from_position = skewed(jnp.take(key_table, key_index, axis=3), col_count, row_count)
    return to_position + jnp.swapaxes(from_position, 2, 3)


def split_einsum(formula, wide_values, narrow_values):
    upper_part = wide_values.astype(jnp.bfloat16)
    lower_part = (wide_values - upper_part.astype(jnp.float32)).astype(jnp.bfloat16)
    return jnp.einsum(
        formula, upper_part, narrow_values, preferred_element_type=jnp.float32
    ) + jnp.einsum(formula, lower_part, narrow_values, preferred_element_type=jnp.float32)


def project(values, weight, bias_vec):
    return jnp.dot(values, weight, preferred_element_type=jnp.float32) + bias_vec.astype(
        jnp.float32
    )


def weight_grad(left_rows, right_rows):
    return jnp.einsum("sbi,sbo->io", left_rows, right_rows, preferred_element_type=jnp.float32)


def bias_grad(grad_rows):
    return jnp.sum(grad_rows.astype(jnp.float32), axis=(0, 1))


def back_through(grad_rows, weight):
    return jnp.einsum("sbo,io->sbi", grad_rows, weight, preferred_element_type=jnp.float32)


def on_device(
    tokens,
    lengths,
    query_weight,
    query_bias,
    key_weight,
    key_bias,
    value_weight,
    value_bias,
    output_weight,
    output_bias,
    first_gain,
    first_bias,
    inner_weight,
    inner_bias,
    outer_weight,
    outer_bias,
    second_gain,
    second_bias,
    relative_table,
    cotangent,
):
    seq_count, row_count, model_width = tokens.shape
    head_dim = model_width // HEADS
    rel_count = relative_table.shape[0]
    span_half = rel_count // 2
    score_scale = 1.0 / math.sqrt(3.0 * head_dim)
    block_count = lax.axis_size("blk")
    block_index = lax.axis_index("blk")
    first_row = block_index * row_count
    query_rows = project(tokens, query_weight, query_bias).astype(jnp.bfloat16)
    key_rows = project(tokens, key_weight, key_bias).astype(jnp.bfloat16)
    value_rows = project(tokens, value_weight, value_bias).astype(jnp.bfloat16)
    rel_keys = (
        project(relative_table, key_weight, key_bias)
        .astype(jnp.bfloat16)
        .reshape(rel_count, HEADS, head_dim)
    )
    rel_queries = (
        project(relative_table, query_weight, query_bias)
        .astype(jnp.bfloat16)
        .reshape(rel_count, HEADS, head_dim)
    )
    query_heads = query_rows.reshape(seq_count, row_count, HEADS, head_dim)
    query_table = jnp.einsum(
        "sihd,rhd->shir", query_heads, rel_keys, preferred_element_type=jnp.float32
    )

    def block_scores(key_block, offset, with_pull):
        block_len = key_block.shape[1]
        key_heads = key_block.reshape(seq_count, block_len, HEADS, head_dim)
        content = jnp.einsum(
            "sihd,sjhd->shij", query_heads, key_heads, preferred_element_type=jnp.float32
        )
        key_table = jnp.einsum(
            "sjhd,rhd->shjr", key_heads, rel_queries, preferred_element_type=jnp.float32
        )
        band_shift = first_row - offset + span_half
        if with_pull:
            band_part, band_pull = jax.vjp(
                lambda left_table, right_table: band_terms(left_table, right_table, band_shift),
                query_table,
                key_table,
            )
        else:
            band_part = band_terms(query_table, key_table, band_shift)
            band_pull = None
        key_mask = (offset + jnp.arange(block_len, dtype=jnp.int32))[None, :] < lengths[:, None]
        key_mask = key_mask[:, None, None, :]
        scores = jnp.where(key_mask, (content + band_part) * score_scale, -1e30)
        return (scores, key_mask, key_heads, band_pull)

    block_ids = jnp.arange(block_count, dtype=jnp.int32)
    running_max = jnp.full((seq_count, HEADS, row_count), -1e30, jnp.float32)
    scores, key_mask, key_heads, unused_pull = block_scores(
        lax.all_gather(key_rows, "blk", axis=1, tiled=True), jnp.int32(0), False
    )
    next_max = jnp.maximum(running_max, jnp.max(scores, axis=-1))
    weights_now = jnp.where(key_mask, jnp.exp(scores - next_max[..., None]), 0.0)
    denominator = jnp.sum(weights_now, axis=-1)
    running_max, denominator = (next_max, denominator)
    log_total = running_max + jnp.log(denominator)
    scores, key_mask, key_heads, unused_pull = block_scores(
        lax.all_gather(key_rows, "blk", axis=1, tiled=True), jnp.int32(0), False
    )
    value_heads = lax.all_gather(value_rows, "blk", axis=1, tiled=True).reshape(key_heads.shape)
    chances = jnp.where(key_mask, jnp.exp(scores - log_total[..., None]), 0.0)
    weighted = jnp.einsum(
        "shij,sjhd->shid",
        chances.astype(jnp.bfloat16),
        value_heads,
        preferred_element_type=jnp.float32,
    )
    mixture = jnp.transpose(weighted, (0, 2, 1, 3)).reshape(seq_count, row_count, model_width)
    mixture_low = mixture.astype(jnp.bfloat16)
    branch_out = project(mixture_low, output_weight, output_bias)
    first_sum = tokens.astype(jnp.float32) + branch_out
    normed_f, first_pull = jax.vjp(
        layer_norm, first_sum, first_gain.astype(jnp.float32), first_bias.astype(jnp.float32)
    )
    normed = normed_f.astype(jnp.bfloat16)
    inner_pre = project(normed, inner_weight, inner_bias)
    active_f, gelu_pull = jax.vjp(partial(jax.nn.gelu, approximate=False), inner_pre)
    active = active_f.astype(jnp.bfloat16)
    outer_out = project(active, outer_weight, outer_bias)
    second_sum = normed.astype(jnp.float32) + outer_out
    result_f, second_pull = jax.vjp(
        layer_norm, second_sum, second_gain.astype(jnp.float32), second_bias.astype(jnp.float32)
    )
    grad_second, g_second_gain, g_second_bias = second_pull(cotangent.astype(jnp.float32))
    grad_outer = grad_second.astype(jnp.bfloat16)
    g_outer_weight = weight_grad(active, grad_outer)
    g_outer_bias = bias_grad(grad_outer)
    grad_inner = gelu_pull(back_through(grad_outer, outer_weight))[0].astype(jnp.bfloat16)
    g_inner_weight = weight_grad(normed, grad_inner)
    g_inner_bias = bias_grad(grad_inner)
    grad_normed = (back_through(grad_inner, inner_weight) + grad_second).astype(jnp.bfloat16)
    grad_first, g_first_gain, g_first_bias = first_pull(grad_normed.astype(jnp.float32))
    grad_branch = grad_first.astype(jnp.bfloat16)
    g_output_weight = weight_grad(mixture_low, grad_branch)
    g_output_bias = bias_grad(grad_branch)
    grad_mixture = back_through(grad_branch, output_weight).astype(jnp.bfloat16)
    grad_heads = grad_mixture.reshape(seq_count, row_count, HEADS, head_dim)
    row_delta = jnp.transpose(
        jnp.sum(grad_heads.astype(jnp.float32) * mixture.reshape(grad_heads.shape), axis=-1),
        (0, 2, 1),
    )
    key_all, value_all = (
        lax.all_gather(key_rows, "blk", axis=1, tiled=True),
        lax.all_gather(value_rows, "blk", axis=1, tiled=True),
    )

    def back_step(running, block_id):
        grad_query, grad_table, grad_rel_query = running
        offset = block_id * row_count
        key_block = lax.dynamic_slice_in_dim(key_all, offset, row_count, 1)
        value_block = lax.dynamic_slice_in_dim(value_all, offset, row_count, 1)
        scores, key_mask, key_heads, band_pull = block_scores(key_block, offset, True)
        value_heads = value_block.reshape(key_heads.shape)
        chances = jnp.where(key_mask, jnp.exp(scores - log_total[..., None]), 0.0)
        grad_chances = jnp.einsum(
            "sihd,sjhd->shij", grad_heads, value_heads, preferred_element_type=jnp.float32
        )
        grad_scores = (chances * (grad_chances - row_delta[..., None])).astype(jnp.bfloat16)
        grad_values = jnp.einsum(
            "shij,sihd->sjhd",
            chances.astype(jnp.bfloat16),
            grad_heads,
            preferred_element_type=jnp.float32,
        )
        grad_query = grad_query + score_scale * jnp.einsum(
            "shij,sjhd->sihd", grad_scores, key_heads, preferred_element_type=jnp.float32
        )
        grad_keys = score_scale * jnp.einsum(
            "shij,sihd->sjhd", grad_scores, query_heads, preferred_element_type=jnp.float32
        )
        grad_qtab, grad_ktab = band_pull(grad_scores.astype(jnp.float32) * score_scale)
        grad_keys = grad_keys + split_einsum("shjr,rhd->sjhd", grad_ktab, rel_queries)
        grad_rel_query = grad_rel_query + split_einsum("shjr,sjhd->rhd", grad_ktab, key_heads)
        new_state = (grad_query, grad_table + grad_qtab, grad_rel_query)
        return (
            new_state,
            (
                grad_keys.reshape(seq_count, row_count, model_width),
                grad_values.reshape(seq_count, row_count, model_width),
            ),
        )

    back_start = (
        jnp.zeros((seq_count, row_count, HEADS, head_dim), jnp.float32),
        jnp.zeros((seq_count, HEADS, row_count, rel_count), jnp.float32),
        jnp.zeros((rel_count, HEADS, head_dim), jnp.float32),
    )
    back_state, block_grads = lax.scan(back_step, back_start, block_ids)
    key_parts, value_parts = block_grads
    key_home, value_home = (
        lax.psum_scatter(
            key_parts.astype(jnp.bfloat16), "blk", scatter_dimension=0, tiled=True
        ).astype(jnp.float32),
        lax.psum_scatter(
            value_parts.astype(jnp.bfloat16), "blk", scatter_dimension=0, tiled=True
        ).astype(jnp.float32),
    )
    key_home_rows = key_home[0]
    value_home_rows = value_home[0]
    grad_query, grad_table, grad_rel_query = back_state
    grad_key_rows = key_home_rows.astype(jnp.bfloat16)
    grad_value_rows = value_home_rows.astype(jnp.bfloat16)
    grad_query = grad_query + split_einsum("shir,rhd->sihd", grad_table, rel_keys)
    grad_rel_key = split_einsum("shir,sihd->rhd", grad_table, query_heads)
    grad_query_rows = grad_query.reshape(seq_count, row_count, model_width).astype(jnp.bfloat16)
    rel_key_flat = grad_rel_key.reshape(rel_count, model_width)
    rel_query_flat = grad_rel_query.reshape(rel_count, model_width)
    g_query_weight = weight_grad(tokens, grad_query_rows) + split_einsum(
        "ro,ri->io", rel_query_flat, relative_table
    )
    g_query_bias = bias_grad(grad_query_rows) + jnp.sum(rel_query_flat, axis=0)
    g_key_weight = weight_grad(tokens, grad_key_rows) + split_einsum(
        "ro,ri->io", rel_key_flat, relative_table
    )
    g_key_bias = bias_grad(grad_key_rows) + jnp.sum(rel_key_flat, axis=0)
    g_value_weight = weight_grad(tokens, grad_value_rows)
    g_value_bias = bias_grad(grad_value_rows)
    g_relative = split_einsum("ro,io->ri", rel_query_flat, query_weight) + split_einsum(
        "ro,io->ri", rel_key_flat, key_weight
    )
    grad_tokens = (
        back_through(grad_query_rows, query_weight)
        + back_through(grad_key_rows, key_weight)
        + back_through(grad_value_rows, value_weight)
        + grad_first
    )
    (
        g_query_weight,
        g_query_bias,
        g_key_weight,
        g_key_bias,
        g_value_weight,
        g_value_bias,
        g_output_weight,
        g_output_bias,
        g_first_gain,
        g_first_bias,
        g_inner_weight,
        g_inner_bias,
        g_outer_weight,
        g_outer_bias,
        g_second_gain,
        g_second_bias,
        g_relative,
    ) = lax.psum(
        (
            g_query_weight,
            g_query_bias,
            g_key_weight,
            g_key_bias,
            g_value_weight,
            g_value_bias,
            g_output_weight,
            g_output_bias,
            g_first_gain,
            g_first_bias,
            g_inner_weight,
            g_inner_bias,
            g_outer_weight,
            g_outer_bias,
            g_second_gain,
            g_second_bias,
            g_relative,
        ),
        ("blk", "dp"),
    )
    return (
        result_f,
        grad_tokens,
        g_query_weight,
        g_query_bias,
        g_key_weight,
        g_key_bias,
        g_value_weight,
        g_value_bias,
        g_output_weight,
        g_output_bias,
        g_first_gain,
        g_first_bias,
        g_inner_weight,
        g_inner_bias,
        g_outer_weight,
        g_outer_bias,
        g_second_gain,
        g_second_bias,
        g_relative,
    )


def solution(mesh):
    in_specs = (
        P("dp", "blk", None),
        P("dp"),
        P(),
        P(),
        P(),
        P(),
        P(),
        P(),
        P(),
        P(),
        P(),
        P(),
        P(),
        P(),
        P(),
        P(),
        P(),
        P(),
        P(),
        P("dp", "blk", None),
    )
    out_specs = (
        P("dp", "blk", None),
        P("dp", "blk", None),
        P(),
        P(),
        P(),
        P(),
        P(),
        P(),
        P(),
        P(),
        P(),
        P(),
        P(),
        P(),
        P(),
        P(),
        P(),
        P(),
        P(),
    )
    return jax.shard_map(
        on_device, mesh=mesh, in_specs=in_specs, out_specs=out_specs, check_vma=False
    )
```

profile of v0, /device:TPU:0, one launch (start us, length us, event | category | flops | bytes accessed | tf_op | source)
XLA Modules:
  0.0 3081.3 jit_solution(16359634714843966742)
XLA Ops:
  17.2 10.5 all-gather.1
  30.0 9.2 all-gather
  46.9 17.9 copy.85
  64.8 37.9 %gather_fusion.3 = f32[1279,6,1024]{2,1,0:T(8,128)} fusion(f32[6,1024,512]{1,0,2:T(8,128)} %copy.85, s32[2048]{0:T(1024)S(1)} %pad_clamp_fusion.2), kind=kCustom, calls=%fused_computation.1.clone | custom fusion | bytes 62870524 | tf_op jit(solution)/shard_map/jit(_take)/gather | solution.py:34
  102.7 29.3 bitcast_select_fusion.2
  132.0 38.5 %copy.111 = f32[1,6,1024,1279]{3,2,0,1:T(8,128)} copy(f32[1,6,1024,1279]{2,1,3,0:T(8,128)} %bitcast_select_fusion.2) | data formatting | bytes 62865408
  170.4 21.6 pad.75.clone
  192.1 60.8 %reshape.862 = f32[1,6,1310720]{2,0,1:T(1,128)} reshape(f32[1,6,1024,1280]{3,2,0,1:T(8,128)} %pad.75.clone) | data formatting | bytes 62914560 | tf_op jit(solution)/shard_map/reshape | solution.py:21
  252.9 344.2 %slice_reduce_fusion.2 = f32[6,1309696]{1,0:T(8,128)} fusion(f32[1,6,1310720]{2,0,1:T(1,128)} %reshape.862), kind=kLoop, calls=%fused_computation.65 | loop fusion | bytes 62865408 | tf_op jit(solution)/shard_map/slice | solution.py:22
  597.1 597.2 %while.25 = (u32[]{:T(128)}, f32[1,6,1309696]{2,1,0:T(8,128)}, f32[7858176]{0:T(1024)}, u32[]{}, f32[]{:T(128)}, /*index=5*/u32[]{}, u32[]{}, u32[]{}) while((u32[]{:T(128)}, f32[1,6,1309696]{2,1,0:T(8,128)}, f32[7858176]{0:T(1024)}, u32[]{}, f32[]{:T(128)}, /*index=5*/u32[]{}, u32[]{}, u32[]{}) %tuple.106), condition=%wide.cond, body=%wide.body.sunk | while | flops 9 | bytes 20955336
  597.8 54.1 %dynamic-slice_reduce_fusion.2 = f32[1309696]{0:T(1024)} fusion(f32[]{:T(128)} %broadcast.449, f32[1,6,1309696]{2,1,0:T(8,128)} %get-tuple-element.749, u32[]{:T(128)S(6)} %multiply.58, u32[]{:T(128)S(6)} %multiply.59), kind=kLoop, calls=%fused_computation.219.clone.1 | loop fusion | bytes 10477580
  652.0 44.7 %dynamic-update-slice.2 = f32[7858176]{0:T(1024)} dynamic-update-slice(f32[7858176]{0:T(1024)} %get-tuple-element.742, f32[1309696]{0:T(1024)} %dynamic-slice_reduce_fusion.2, u32[]{:T(128)S(6)} %add.807) | dynamic-update-slice | bytes 10477572
  697.2 54.1 %dynamic-slice_reduce_fusion.2 = f32[1309696]{0:T(1024)} fusion(f32[]{:T(128)} %broadcast.449, f32[1,6,1309696]{2,1,0:T(8,128)} %get-tuple-element.749, u32[]{:T(128)S(6)} %multiply.58, u32[]{:T(128)S(6)} %multiply.59), kind=kLoop, calls=%fused_computation.219.clone.1 | loop fusion | bytes 10477580
  751.3 44.8 %dynamic-update-slice.2 = f32[7858176]{0:T(1024)} dynamic-update-slice(f32[7858176]{0:T(1024)} %get-tuple-element.742, f32[1309696]{0:T(1024)} %dynamic-slice_reduce_fusion.2, u32[]{:T(128)S(6)} %add.807) | dynamic-update-slice | bytes 10477572
  796.7 54.1 %dynamic-slice_reduce_fusion.2 = f32[1309696]{0:T(1024)} fusion(f32[]{:T(128)} %broadcast.449, f32[1,6,1309696]{2,1,0:T(8,128)} %get-tuple-element.749, u32[]{:T(128)S(6)} %multiply.58, u32[]{:T(128)S(6)} %multiply.59), kind=kLoop, calls=%fused_computation.219.clone.1 | loop fusion | bytes 10477580
  850.8 44.8 %dynamic-update-slice.2 = f32[7858176]{0:T(1024)} dynamic-update-slice(f32[7858176]{0:T(1024)} %get-tuple-element.742, f32[1309696]{0:T(1024)} %dynamic-slice_reduce_fusion.2, u32[]{:T(128)S(6)} %add.807) | dynamic-update-slice | bytes 10477572
  896.2 54.1 %dynamic-slice_reduce_fusion.2 = f32[1309696]{0:T(1024)} fusion(f32[]{:T(128)} %broadcast.449, f32[1,6,1309696]{2,1,0:T(8,128)} %get-tuple-element.749, u32[]{:T(128)S(6)} %multiply.58, u32[]{:T(128)S(6)} %multiply.59), kind=kLoop, calls=%fused_computation.219.clone.1 | loop fusion | bytes 10477580
  950.3 44.9 %dynamic-update-slice.2 = f32[7858176]{0:T(1024)} dynamic-update-slice(f32[7858176]{0:T(1024)} %get-tuple-element.742, f32[1309696]{0:T(1024)} %dynamic-slice_reduce_fusion.2, u32[]{:T(128)S(6)} %add.807) | dynamic-update-slice | bytes 10477572
  995.7 54.1 %dynamic-slice_reduce_fusion.2 = f32[1309696]{0:T(1024)} fusion(f32[]{:T(128)} %broadcast.449, f32[1,6,1309696]{2,1,0:T(8,128)} %get-tuple-element.749, u32[]{:T(128)S(6)} %multiply.58, u32[]{:T(128)S(6)} %multiply.59), kind=kLoop, calls=%fused_computation.219.clone.1 | loop fusion | bytes 10477580
  1049.9 44.9 %dynamic-update-slice.2 = f32[7858176]{0:T(1024)} dynamic-update-slice(f32[7858176]{0:T(1024)} %get-tuple-element.742, f32[1309696]{0:T(1024)} %dynamic-slice_reduce_fusion.2, u32[]{:T(128)S(6)} %add.807) | dynamic-update-slice | bytes 10477572
  1095.3 54.1 %dynamic-slice_reduce_fusion.2 = f32[1309696]{0:T(1024)} fusion(f32[]{:T(128)} %broadcast.449, f32[1,6,1309696]{2,1,0:T(8,128)} %get-tuple-element.749, u32[]{:T(128)S(6)} %multiply.58, u32[]{:T(128)S(6)} %multiply.59), kind=kLoop, calls=%fused_computation.219.clone.1 | loop fusion | bytes 10477580
  1149.4 44.9 %dynamic-update-slice.2 = f32[7858176]{0:T(1024)} dynamic-update-slice(f32[7858176]{0:T(1024)} %get-tuple-element.742, f32[1309696]{0:T(1024)} %dynamic-slice_reduce_fusion.2, u32[]{:T(128)S(6)} %add.807) | dynamic-update-slice | bytes 10477572
  1194.3 61.2 %reshape.993 = f32[6,1,1024,1279]{3,2,1,0:T(8,128)} reshape(f32[7858176]{0:T(1024)} %get-tuple-element.501) | data formatting | bytes 62865408
  1273.7 10.2 gather_fusion.2
  1284.0 11.8 bitcast_select_fusion.3
  1295.8 10.7 copy.112
  1313.7 11.5 reshape.859
  1325.2 87.7 %slice_reduce_fusion.3 = f32[6,327424]{1,0:T(8,128)} fusion(f32[1,6,327680]{2,0,1:T(1,128)} %reshape.859), kind=kLoop, calls=%fused_computation.67 | loop fusion | bytes 15716352 | tf_op jit(solution)/shard_map/slice | solution.py:22
  1412.9 15.9 reshape.860
  1462.8 1364.8 %while.24 = (s32[]{:T(128)}, f32[1,256,6,64]{1,3,2,0:T(8,128)}, f32[1,6,256,512]{2,1,3,0:T(8,128)}, f32[512,6,64]{0,2,1:T(8,128)}, bf16[4,1,256,384]{2,3,1,0:T(8...) while((s32[]{:T(128)}, f32[1,256,6,64]{1,3,2,0:T(8,128)}, ...), condition=%wide.region_14.18_spmd.clone, body=%wide.region_11.17_spmd.clone.sunk | while | flops 768058880 | bytes 276986912 | solution.py:237
  1491.5 11.4 slice_reduce_fusion.6
  1545.9 11.4 slice_reduce_fusion.7
  1576.9 8.0 reshape.1020
  1584.9 11.5 pad_reduce_fusion.4
  1607.5 62.9 %scatter_fusion = f32[6,256,512]{1,0,2:T(8,128)} fusion(f32[6,256,512]{1,0,2:T(8,128)} %bitcast.495, s32[511]{0:T(512)S(1)} %compare_select_fusion.6, f32[511,6,256]{2,1,0:T(8,128)} %copy.140), kind=kCustom, calls=%fused_computation.4.clone.clone.1 | custom fusion | flops 784896 | bytes 9420796 | tf_op jit(solution)/shard_map/while/body/eval_jaxpr/transpose(jvp(jit(_take)))/scatter-add | solution.py:32
  1672.5 8.0 reshape.1021
  1680.5 11.5 pad_reduce_fusion.5
  1705.7 63.0 %scatter_fusion.1 = f32[6,256,512]{1,0,2:T(8,128)} fusion(f32[6,256,512]{1,0,2:T(8,128)} %broadcast.448, s32[511]{0:T(512)S(1)} %compare_select_fusion.7, f32[511,6,256]{2,1,0:T(8,128)} %copy.142), kind=kCustom, calls=%fused_computation.5.clone.clone.1 | custom fusion | flops 784896 | bytes 9420796 | tf_op jit(solution)/shard_map/while/body/eval_jaxpr/transpose(jvp(jit(_take)))/scatter-add | solution.py:34
  1821.0 11.4 slice_reduce_fusion.6
  1875.3 11.4 slice_reduce_fusion.7
  1907.3 8.0 reshape.1020
  1915.3 11.5 pad_reduce_fusion.4
  1937.9 66.6 %scatter_fusion = f32[6,256,512]{1,0,2:T(8,128)} fusion(f32[6,256,512]{1,0,2:T(8,128)} %bitcast.495, s32[511]{0:T(512)S(1)} %compare_select_fusion.6, f32[511,6,256]{2,1,0:T(8,128)} %copy.140), kind=kCustom, calls=%fused_computation.4.clone.clone.1 | custom fusion | flops 784896 | bytes 9420796 | tf_op jit(solution)/shard_map/while/body/eval_jaxpr/transpose(jvp(jit(_take)))/scatter-add | solution.py:32
  2006.6 8.0 reshape.1021
  2014.6 11.5 pad_reduce_fusion.5
  2039.7 66.7 %scatter_fusion.1 = f32[6,256,512]{1,0,2:T(8,128)} fusion(f32[6,256,512]{1,0,2:T(8,128)} %broadcast.448, s32[511]{0:T(512)S(1)} %compare_select_fusion.7, f32[511,6,256]{2,1,0:T(8,128)} %copy.142), kind=kCustom, calls=%fused_computation.5.clone.clone.1 | custom fusion | flops 784896 | bytes 9420796 | tf_op jit(solution)/shard_map/while/body/eval_jaxpr/transpose(jvp(jit(_take)))/scatter-add | solution.py:34
  2158.9 11.4 slice_reduce_fusion.6
  2213.3 11.4 slice_reduce_fusion.7
  2245.3 8.0 reshape.1020
  2253.3 11.5 pad_reduce_fusion.4
  2275.9 70.0 %scatter_fusion = f32[6,256,512]{1,0,2:T(8,128)} fusion(f32[6,256,512]{1,0,2:T(8,128)} %bitcast.495, s32[511]{0:T(512)S(1)} %compare_select_fusion.6, f32[511,6,256]{2,1,0:T(8,128)} %copy.140), kind=kCustom, calls=%fused_computation.4.clone.clone.1 | custom fusion | flops 784896 | bytes 9420796 | tf_op jit(solution)/shard_map/while/body/eval_jaxpr/transpose(jvp(jit(_take)))/scatter-add | solution.py:32
  2356.0 11.5 pad_reduce_fusion.5
  2381.1 70.3 %scatter_fusion.1 = f32[6,256,512]{1,0,2:T(8,128)} fusion(f32[6,256,512]{1,0,2:T(8,128)} %broadcast.448, s32[511]{0:T(512)S(1)} %compare_select_fusion.7, f32[511,6,256]{2,1,0:T(8,128)} %copy.142), kind=kCustom, calls=%fused_computation.5.clone.clone.1 | custom fusion | flops 784896 | bytes 9420796 | tf_op jit(solution)/shard_map/while/body/eval_jaxpr/transpose(jvp(jit(_take)))/scatter-add | solution.py:34
  2503.9 11.4 slice_reduce_fusion.6
  2558.3 11.4 slice_reduce_fusion.7
  2590.3 8.0 reshape.1020
  2598.3 11.5 pad_reduce_fusion.4
  2620.9 70.0 %scatter_fusion = f32[6,256,512]{1,0,2:T(8,128)} fusion(f32[6,256,512]{1,0,2:T(8,128)} %bitcast.495, s32[511]{0:T(512)S(1)} %compare_select_fusion.6, f32[511,6,256]{2,1,0:T(8,128)} %copy.140), kind=kCustom, calls=%fused_computation.4.clone.clone.1 | custom fusion | flops 784896 | bytes 9420796 | tf_op jit(solution)/shard_map/while/body/eval_jaxpr/transpose(jvp(jit(_take)))/scatter-add | solution.py:32
  2693.0 8.0 reshape.1021
  2701.0 11.5 pad_reduce_fusion.5
  2726.1 70.3 %scatter_fusion.1 = f32[6,256,512]{1,0,2:T(8,128)} fusion(f32[6,256,512]{1,0,2:T(8,128)} %broadcast.448, s32[511]{0:T(512)S(1)} %compare_select_fusion.7, f32[511,6,256]{2,1,0:T(8,128)} %copy.142), kind=kCustom, calls=%fused_computation.5.clone.clone.1 | custom fusion | flops 784896 | bytes 9420796 | tf_op jit(solution)/shard_map/while/body/eval_jaxpr/transpose(jvp(jit(_take)))/scatter-add | solution.py:34
  2860.4 17.9 reduce-scatter.3.cloned.1.call-done
  2881.9 41.9 %all-reduce.8 = (f32[384]{0:T(512)}, f32[384]{0:T(512)}, f32[384]{0:T(512)}, f32[384]{0:T(512)}, f32[384]{0:T(512)}, /*index=5*/f32[384]{0:T(512)}, f32[1536]{0:...) all-reduce(f32[384]{0:T(512)S(1)} %add.515, ...), channel_id=1, replica_groups=mesh['blk'=4,'dp'=8] {'blk','dp'}, use_global_device_ids=true, to_apply=%region_20.24 | all-reduce | flops 4992 | bytes 39936 | tf_op jit(solution)/shard_map/psum | solution.py:294
  2925.2 138.0 %all-reduce.12.cloned.1.call-done = (f32[384,384]{0,1:T(8,128)}, f32[384,384]{0,1:T(8,128)}, f32[384,384]{0,1:T(8,128)}, f32[384,384]{1,0:T(8,128)}, f32[384,153...) async-done(((f32[384,384]{0,1:T(8,128)}, f32[384,384]{0,1:T(8,128)}, f32[384,384]{0,1:T(8,128)}, f32[384,384]{1,0:T(8,128)}, f32[384,1536]{1,0:T(8,128)}, ...) | async-done | bytes 7864336 | tf_op jit(solution)/shard_map/psum | solution.py:294
  (557 shorter events, 703.3 us)
Async XLA Ops:
  7.2 1432.3 %copy-start = (bf16[384,1536]{1,0:T(8,128)(2,1)S(1)}, bf16[384,1536]{1,0:T(8,128)(2,1)}, u32[]{:S(2)}) copy-start(bf16[384,1536]{1,0:T(8,128)(2,1)} %param.40) | copy-start | bytes 3538948
  7.2 5.7 copy-start.15
  7.2 5.3 copy-start.20
  7.2 5.3 copy-start.22
  7.2 2851.1 %reduce-scatter.5.cloned.1.call-start = ((), (), s32[]{:S(2)}) async-start(), calls=%async_computation.3 | async-start | bytes 983040 | tf_op jit(solution)/shard_map/reduce_scatter | solution.py:243
  10.2 4.9 copy-start.81
  10.2 5.5 copy-start.79
  10.2 6.1 copy-start.82
  10.2 6.7 copy-start.83
  10.2 6.7 copy-start.42
  13.0 27.6 copy-start.6
  40.5 6.4 copy-start.18
  1261.8 7.1 copy-start.48
  1261.8 7.3 copy-start.25
  1269.7 4.0 copy-start.11
  1269.7 4.0 copy-start.58
  1273.7 10.2 copy-start.67
  1412.9 16.5 copy-start.19
  1437.4 7.5 copy-start.68
  1437.4 19.9 copy-start.59
  1438.8 6.1 copy-start.51
  1439.3 18.1 copy-start.13
  1439.3 18.1 copy-start.61
  1439.5 17.9 copy-start.63
  1439.5 5.4 copy-start.80
  1439.5 5.4 copy-start.88
  1446.9 7.6 copy-start.90
  1446.9 7.6 copy-start.91
  1457.7 5.1 copy-start.28
  1457.7 5.1 copy-start.65
  1458.4 4.4 copy-start.37
  1460.5 2.3 copy-start.7
  1460.5 2.3 copy-start.57
  1463.2 7.5 copy-start.8
  1567.0 2.7 copy-start.3
  1607.5 62.9 %copy-start.5 = (f32[1,6,256,256]{3,2,1,0:T(8,128)S(1)}, f32[1,6,256,256]{3,2,1,0:T(8,128)}, u32[]{:S(2)}) copy-start(f32[1,6,256,256]{3,2,1,0:T(8,128)} %get-tuple-element.726) | copy-start | bytes 4718596 | tf_op jit(solution)/shard_map/while
  1784.5 3.0 copy-start.4
  1792.7 7.5 copy-start.8
  1896.4 2.7 copy-start.3
  1937.9 66.6 %copy-start.5 = (f32[1,6,256,256]{3,2,1,0:T(8,128)S(1)}, f32[1,6,256,256]{3,2,1,0:T(8,128)}, u32[]{:S(2)}) copy-start(f32[1,6,256,256]{3,2,1,0:T(8,128)} %get-tuple-element.726) | copy-start | bytes 4718596 | tf_op jit(solution)/shard_map/while
  2122.2 3.3 copy-start.4
  2130.7 7.5 copy-start.8
  2234.4 2.7 copy-start.3
  2275.9 70.0 %copy-start.5 = (f32[1,6,256,256]{3,2,1,0:T(8,128)S(1)}, f32[1,6,256,256]{3,2,1,0:T(8,128)}, u32[]{:S(2)}) copy-start(f32[1,6,256,256]{3,2,1,0:T(8,128)} %get-tuple-element.726) | copy-start | bytes 4718596 | tf_op jit(solution)/shard_map/while
  2467.2 3.3 copy-start.4
  2475.7 7.5 copy-start.8
  2579.4 2.7 copy-start.3
  2620.9 70.0 %copy-start.5 = (f32[1,6,256,256]{3,2,1,0:T(8,128)S(1)}, f32[1,6,256,256]{3,2,1,0:T(8,128)}, u32[]{:S(2)}) copy-start(f32[1,6,256,256]{3,2,1,0:T(8,128)} %get-tuple-element.726) | copy-start | bytes 4718596 | tf_op jit(solution)/shard_map/while
  2812.2 3.3 copy-start.4
  2827.7 50.6 %reduce-scatter.3.cloned.1.call-start = ((), (), s32[]{:S(2)}) async-start(), calls=%async_computation.2 | async-start | bytes 983040 | tf_op jit(solution)/shard_map/reduce_scatter | solution.py:240
  2828.4 234.8 %all-reduce.12.cloned.1.call-start = ((), (), s32[]{:S(2)}) async-start(), calls=%async_computation.4 | async-start | bytes 15728640 | tf_op jit(solution)/shard_map/psum | solution.py:294
  2834.7 3.0 copy-start.26
  2848.8 2.1 copy-start.35
  2854.2 2.1 copy-start.14
  2854.2 2.1 copy-start.31
  2854.2 2.1 copy-start.60
  2880.4 43.8 %copy-start.29 = (f32[1,256,384]{2,1,0:T(8,128)S(1)}, f32[1,256,384]{2,1,0:T(8,128)}, u32[]{:S(2)}) copy-start(f32[1,256,384]{2,1,0:T(8,128)} %copy-done.28) | copy-start | bytes 1179652
  2880.4 43.8 %copy-start.43 = (bf16[384,384]{1,0:T(8,128)(2,1)S(1)}, bf16[384,384]{1,0:T(8,128)(2,1)}, u32[]{:S(2)}) copy-start(bf16[384,384]{1,0:T(8,128)(2,1)} %param.34) | copy-start | bytes 884740
  2880.4 43.8 %copy-start.66 = (f32[256]{0:T(256)S(1)}, f32[256]{0:T(256)}, u32[]{:S(2)}) copy-start(f32[256]{0:T(256)} %copy-done.65) | copy-start | bytes 3076
  3063.2 4.5 copy-start.55
  3063.2 5.5 copy-start.54
  3065.4 4.1 copy-start.33
  3069.5 2.5 copy-start.32
  3072.1 2.6 copy-start.1
  (53 other events, 78.9 us)
Sparse Core Ops, SparseCore 0:
  2827.8 24.4 reduce-scatter.4
  2855.0 23.2 reduce-scatter.2
  2886.4 176.7 all-reduce.11
where the time goes:
time: 3120 us; the launch traced here: 3080 us
  local copies, waits for them, and re-layouts  2040 us (65%)
  other arithmetic  676 us (22%)
  waiting for transfers between devices  157 us (5%)
  matrix products  116 us (4%)
  blocking collectives  61.6 us (2%)
    unnamed x202, local copies, waits for them, and re-layouts  735 us
    slice x10, local copies, waits for them, and re-layouts, skewed(): flattened[..., row_count - 1:row_count - 1 + row_count * table_width]  523 us
    scatter-add x4, other arithmetic, band_terms(): jnp.take(key_table, key_index, axis=3)  270 us
    scatter-add x4, other arithmetic, band_terms(): jnp.take(query_table, query_index, axis=3)  269 us
    psum x1, waiting for transfers between devices, on_device(): lax.psum((g_query_weight, g_query_bias, g_key_weight, g_key_bias, g_value...  138 us
    reshape x17, local copies, waits for them, and re-layouts, skewed(): flattened.reshape(leading + (row_count, table_width))[..., :col_count]  131 us
    reshape x10, local copies, waits for them, and re-layouts, skewed(): flattened = padded.reshape(leading + (row_count * (table_width + 1),))  130 us
    pad x26, local copies, waits for them, and re-layouts, skewed(): jnp.pad(source_table, [(0, 0)] * (source_table.ndim - 1) + [(0, 1)])  120 us
  transfers between devices with their start and end apart: 3, of which 2 were waited for; matrix products, arithmetic and copies ran while one was open for 1% of the time, Pallas kernels for 0%

commit v1 on v0

--- a/solution.py
+++ b/solution.py
@@ -6,6 +6,11 @@
 from jax.sharding import PartitionSpec as P
 
 HEADS = 6
+
+
+def draw_squares(packet):
+    next_value = jax.lax.psum(packet, axis_name="dp")
+    return jax.lax.psum(next_value, axis_name="blk")
 
 
 def layer_norm(values, gain_vec, bias_vec):
@@ -291,7 +296,7 @@
         g_second_gain,
         g_second_bias,
         g_relative,
-    ) = lax.psum(
+    ) = draw_squares(
         (
             g_query_weight,
             g_query_bias,
@@ -310,8 +315,7 @@
             g_second_gain,
             g_second_bias,
             g_relative,
-        ),
-        ("blk", "dp"),
+        )
     )
     return (
         result_f,

time: 3120 us -> 3350 us (1.074)
  waiting for transfers between devices: 157 us -> 381 us
    psum x1 -> x2, waiting for transfers between devices: 138 us -> 362 us  [the longest x1 265 us: draw_squares(): next_value = jax.lax.psum(packet, axis_name='dp')]
  transfers between devices with their start and end apart: 3 -> 4, of which waited for: 2 -> 3; matrix products, arithmetic and copies ran while one was open for 1% -> 1% of each run, Pallas kernels for 0% -> 0%
where the time goes in v1:
time: 3350 us; the launch traced here: 3310 us
  local copies, waits for them, and re-layouts  2040 us (61%)
  other arithmetic  676 us (20%)
  waiting for transfers between devices  381 us (11%)
  matrix products  116 us (3%)
  blocking collectives  67.7 us (2%)
    unnamed x202, local copies, waits for them, and re-layouts  735 us
    slice x10, local copies, waits for them, and re-layouts, skewed(): flattened[..., row_count - 1:row_count - 1 + row_count * table_width]  523 us
    scatter-add x4, other arithmetic, band_terms(): jnp.take(key_table, key_index, axis=3)  270 us
    scatter-add x4, other arithmetic, band_terms(): jnp.take(query_table, query_index, axis=3)  269 us
    psum x1, waiting for transfers between devices, draw_squares(): next_value = jax.lax.psum(packet, axis_name='dp')  265 us
    reshape x17, local copies, waits for them, and re-layouts, skewed(): flattened.reshape(leading + (row_count, table_width))[..., :col_count]  131 us
    reshape x10, local copies, waits for them, and re-layouts, skewed(): flattened = padded.reshape(leading + (row_count * (table_width + 1),))  130 us
    pad x26, local copies, waits for them, and re-layouts, skewed(): jnp.pad(source_table, [(0, 0)] * (source_table.ndim - 1) + [(0, 1)])  120 us
  transfers between devices with their start and end apart: 4, of which 3 were waited for; matrix products, arithmetic and copies ran while one was open for 1% of the time, Pallas kernels for 0%

profile of v1, /device:TPU:0, one launch (start us, length us, event | category | flops | bytes accessed | tf_op | source)
XLA Modules:
  0.0 3311.7 jit_solution(18417227559713901624)
XLA Ops:
  17.2 10.5 all-gather.1
  30.0 9.2 all-gather
  46.9 17.9 copy.85
  64.8 37.9 %gather_fusion.3 = f32[1279,6,1024]{2,1,0:T(8,128)} fusion(f32[6,1024,512]{1,0,2:T(8,128)} %copy.85, s32[2048]{0:T(1024)S(1)} %pad_clamp_fusion.2), kind=kCustom, calls=%fused_computation.1.clone | custom fusion | bytes 62870524 | tf_op jit(solution)/shard_map/jit(_take)/gather | solution.py:39
  102.7 29.3 bitcast_select_fusion.2
  132.0 38.5 %copy.111 = f32[1,6,1024,1279]{3,2,0,1:T(8,128)} copy(f32[1,6,1024,1279]{2,1,3,0:T(8,128)} %bitcast_select_fusion.2) | data formatting | bytes 62865408
  170.4 21.6 pad.75.clone
  192.1 60.8 %reshape.862 = f32[1,6,1310720]{2,0,1:T(1,128)} reshape(f32[1,6,1024,1280]{3,2,0,1:T(8,128)} %pad.75.clone) | data formatting | bytes 62914560 | tf_op jit(solution)/shard_map/reshape | solution.py:26
  252.9 344.2 %slice_reduce_fusion.2 = f32[6,1309696]{1,0:T(8,128)} fusion(f32[1,6,1310720]{2,0,1:T(1,128)} %reshape.862), kind=kLoop, calls=%fused_computation.65 | loop fusion | bytes 62865408 | tf_op jit(solution)/shard_map/slice | solution.py:27
  597.1 597.2 %while.25 = (u32[]{:T(128)}, f32[1,6,1309696]{2,1,0:T(8,128)}, f32[7858176]{0:T(1024)}, u32[]{}, f32[]{:T(128)}, /*index=5*/u32[]{}, u32[]{}, u32[]{}) while((u32[]{:T(128)}, f32[1,6,1309696]{2,1,0:T(8,128)}, f32[7858176]{0:T(1024)}, u32[]{}, f32[]{:T(128)}, /*index=5*/u32[]{}, u32[]{}, u32[]{}) %tuple.109), condition=%wide.cond, body=%wide.body.sunk | while | flops 9 | bytes 20955336
  597.8 54.1 %dynamic-slice_reduce_fusion.2 = f32[1309696]{0:T(1024)} fusion(f32[]{:T(128)} %broadcast.449, f32[1,6,1309696]{2,1,0:T(8,128)} %get-tuple-element.766, u32[]{:T(128)S(6)} %multiply.58, u32[]{:T(128)S(6)} %multiply.59), kind=kLoop, calls=%fused_computation.219.clone.1 | loop fusion | bytes 10477580
  652.0 44.7 %dynamic-update-slice.2 = f32[7858176]{0:T(1024)} dynamic-update-slice(f32[7858176]{0:T(1024)} %get-tuple-element.759, f32[1309696]{0:T(1024)} %dynamic-slice_reduce_fusion.2, u32[]{:T(128)S(6)} %add.841) | dynamic-update-slice | bytes 10477572
  697.2 54.1 %dynamic-slice_reduce_fusion.2 = f32[1309696]{0:T(1024)} fusion(f32[]{:T(128)} %broadcast.449, f32[1,6,1309696]{2,1,0:T(8,128)} %get-tuple-element.766, u32[]{:T(128)S(6)} %multiply.58, u32[]{:T(128)S(6)} %multiply.59), kind=kLoop, calls=%fused_computation.219.clone.1 | loop fusion | bytes 10477580
  751.3 44.8 %dynamic-update-slice.2 = f32[7858176]{0:T(1024)} dynamic-update-slice(f32[7858176]{0:T(1024)} %get-tuple-element.759, f32[1309696]{0:T(1024)} %dynamic-slice_reduce_fusion.2, u32[]{:T(128)S(6)} %add.841) | dynamic-update-slice | bytes 10477572
  796.7 54.1 %dynamic-slice_reduce_fusion.2 = f32[1309696]{0:T(1024)} fusion(f32[]{:T(128)} %broadcast.449, f32[1,6,1309696]{2,1,0:T(8,128)} %get-tuple-element.766, u32[]{:T(128)S(6)} %multiply.58, u32[]{:T(128)S(6)} %multiply.59), kind=kLoop, calls=%fused_computation.219.clone.1 | loop fusion | bytes 10477580
  850.8 44.8 %dynamic-update-slice.2 = f32[7858176]{0:T(1024)} dynamic-update-slice(f32[7858176]{0:T(1024)} %get-tuple-element.759, f32[1309696]{0:T(1024)} %dynamic-slice_reduce_fusion.2, u32[]{:T(128)S(6)} %add.841) | dynamic-update-slice | bytes 10477572
  896.2 54.1 %dynamic-slice_reduce_fusion.2 = f32[1309696]{0:T(1024)} fusion(f32[]{:T(128)} %broadcast.449, f32[1,6,1309696]{2,1,0:T(8,128)} %get-tuple-element.766, u32[]{:T(128)S(6)} %multiply.58, u32[]{:T(128)S(6)} %multiply.59), kind=kLoop, calls=%fused_computation.219.clone.1 | loop fusion | bytes 10477580
  950.3 44.9 %dynamic-update-slice.2 = f32[7858176]{0:T(1024)} dynamic-update-slice(f32[7858176]{0:T(1024)} %get-tuple-element.759, f32[1309696]{0:T(1024)} %dynamic-slice_reduce_fusion.2, u32[]{:T(128)S(6)} %add.841) | dynamic-update-slice | bytes 10477572
  995.7 54.1 %dynamic-slice_reduce_fusion.2 = f32[1309696]{0:T(1024)} fusion(f32[]{:T(128)} %broadcast.449, f32[1,6,1309696]{2,1,0:T(8,128)} %get-tuple-element.766, u32[]{:T(128)S(6)} %multiply.58, u32[]{:T(128)S(6)} %multiply.59), kind=kLoop, calls=%fused_computation.219.clone.1 | loop fusion | bytes 10477580
  1049.9 44.9 %dynamic-update-slice.2 = f32[7858176]{0:T(1024)} dynamic-update-slice(f32[7858176]{0:T(1024)} %get-tuple-element.759, f32[1309696]{0:T(1024)} %dynamic-slice_reduce_fusion.2, u32[]{:T(128)S(6)} %add.841) | dynamic-update-slice | bytes 10477572
  1095.3 54.1 %dynamic-slice_reduce_fusion.2 = f32[1309696]{0:T(1024)} fusion(f32[]{:T(128)} %broadcast.449, f32[1,6,1309696]{2,1,0:T(8,128)} %get-tuple-element.766, u32[]{:T(128)S(6)} %multiply.58, u32[]{:T(128)S(6)} %multiply.59), kind=kLoop, calls=%fused_computation.219.clone.1 | loop fusion | bytes 10477580
  1149.4 44.9 %dynamic-update-slice.2 = f32[7858176]{0:T(1024)} dynamic-update-slice(f32[7858176]{0:T(1024)} %get-tuple-element.759, f32[1309696]{0:T(1024)} %dynamic-slice_reduce_fusion.2, u32[]{:T(128)S(6)} %add.841) | dynamic-update-slice | bytes 10477572
  1194.3 61.2 %reshape.993 = f32[6,1,1024,1279]{3,2,1,0:T(8,128)} reshape(f32[7858176]{0:T(1024)} %get-tuple-element.501) | data formatting | bytes 62865408
  1273.7 10.2 gather_fusion.2
  1284.0 11.8 bitcast_select_fusion.3
  1295.8 10.7 copy.112
  1313.7 11.5 reshape.859
  1325.2 87.7 %slice_reduce_fusion.3 = f32[6,327424]{1,0:T(8,128)} fusion(f32[1,6,327680]{2,0,1:T(1,128)} %reshape.859), kind=kLoop, calls=%fused_computation.67 | loop fusion | bytes 15716352 | tf_op jit(solution)/shard_map/slice | solution.py:27
  1412.9 15.9 reshape.860
  1462.8 1364.8 %while.24 = (s32[]{:T(128)}, f32[1,256,6,64]{1,3,2,0:T(8,128)}, f32[1,6,256,512]{2,1,3,0:T(8,128)}, f32[512,6,64]{0,2,1:T(8,128)}, bf16[4,1,256,384]{2,3,1,0:T(8...) while((s32[]{:T(128)}, f32[1,256,6,64]{1,3,2,0:T(8,128)}, ...), condition=%wide.region_14.18_spmd.clone, body=%wide.region_11.17_spmd.clone.sunk | while | flops 768058880 | bytes 276986912 | solution.py:242
  1491.5 11.4 slice_reduce_fusion.6
  1545.8 11.4 slice_reduce_fusion.7
  1576.8 8.0 reshape.1020
  1584.8 11.5 pad_reduce_fusion.4
  1607.5 62.9 %scatter_fusion = f32[6,256,512]{1,0,2:T(8,128)} fusion(f32[6,256,512]{1,0,2:T(8,128)} %bitcast.495, s32[511]{0:T(512)S(1)} %compare_select_fusion.6, f32[511,6,256]{2,1,0:T(8,128)} %copy.140), kind=kCustom, calls=%fused_computation.4.clone.clone.1 | custom fusion | flops 784896 | bytes 9420796 | tf_op jit(solution)/shard_map/while/body/eval_jaxpr/transpose(jvp(jit(_take)))/scatter-add | solution.py:37
  1672.5 8.0 reshape.1021
  1680.5 11.5 pad_reduce_fusion.5
  1705.6 63.0 %scatter_fusion.1 = f32[6,256,512]{1,0,2:T(8,128)} fusion(f32[6,256,512]{1,0,2:T(8,128)} %broadcast.448, s32[511]{0:T(512)S(1)} %compare_select_fusion.7, f32[511,6,256]{2,1,0:T(8,128)} %copy.142), kind=kCustom, calls=%fused_computation.5.clone.clone.1 | custom fusion | flops 784896 | bytes 9420796 | tf_op jit(solution)/shard_map/while/body/eval_jaxpr/transpose(jvp(jit(_take)))/scatter-add | solution.py:39
  1821.0 11.4 slice_reduce_fusion.6
  1875.3 11.4 slice_reduce_fusion.7
  1915.3 11.5 pad_reduce_fusion.4
  1937.9 66.6 %scatter_fusion = f32[6,256,512]{1,0,2:T(8,128)} fusion(f32[6,256,512]{1,0,2:T(8,128)} %bitcast.495, s32[511]{0:T(512)S(1)} %compare_select_fusion.6, f32[511,6,256]{2,1,0:T(8,128)} %copy.140), kind=kCustom, calls=%fused_computation.4.clone.clone.1 | custom fusion | flops 784896 | bytes 9420796 | tf_op jit(solution)/shard_map/while/body/eval_jaxpr/transpose(jvp(jit(_take)))/scatter-add | solution.py:37
  2014.6 11.5 pad_reduce_fusion.5
  2039.7 66.7 %scatter_fusion.1 = f32[6,256,512]{1,0,2:T(8,128)} fusion(f32[6,256,512]{1,0,2:T(8,128)} %broadcast.448, s32[511]{0:T(512)S(1)} %compare_select_fusion.7, f32[511,6,256]{2,1,0:T(8,128)} %copy.142), kind=kCustom, calls=%fused_computation.5.clone.clone.1 | custom fusion | flops 784896 | bytes 9420796 | tf_op jit(solution)/shard_map/while/body/eval_jaxpr/transpose(jvp(jit(_take)))/scatter-add | solution.py:39
  2158.9 11.4 slice_reduce_fusion.6
  2213.3 11.4 slice_reduce_fusion.7
  2245.3 8.0 reshape.1020
  2253.3 11.5 pad_reduce_fusion.4
  2275.9 70.0 %scatter_fusion = f32[6,256,512]{1,0,2:T(8,128)} fusion(f32[6,256,512]{1,0,2:T(8,128)} %bitcast.495, s32[511]{0:T(512)S(1)} %compare_select_fusion.6, f32[511,6,256]{2,1,0:T(8,128)} %copy.140), kind=kCustom, calls=%fused_computation.4.clone.clone.1 | custom fusion | flops 784896 | bytes 9420796 | tf_op jit(solution)/shard_map/while/body/eval_jaxpr/transpose(jvp(jit(_take)))/scatter-add | solution.py:37
  2348.0 8.0 reshape.1021
  2356.0 11.5 pad_reduce_fusion.5
  2381.1 70.3 %scatter_fusion.1 = f32[6,256,512]{1,0,2:T(8,128)} fusion(f32[6,256,512]{1,0,2:T(8,128)} %broadcast.448, s32[511]{0:T(512)S(1)} %compare_select_fusion.7, f32[511,6,256]{2,1,0:T(8,128)} %copy.142), kind=kCustom, calls=%fused_computation.5.clone.clone.1 | custom fusion | flops 784896 | bytes 9420796 | tf_op jit(solution)/shard_map/while/body/eval_jaxpr/transpose(jvp(jit(_take)))/scatter-add | solution.py:39
  2503.9 11.4 slice_reduce_fusion.6
  2558.3 11.4 slice_reduce_fusion.7
  2590.3 8.0 reshape.1020
  2598.3 11.5 pad_reduce_fusion.4
  2620.9 70.0 %scatter_fusion = f32[6,256,512]{1,0,2:T(8,128)} fusion(f32[6,256,512]{1,0,2:T(8,128)} %bitcast.495, s32[511]{0:T(512)S(1)} %compare_select_fusion.6, f32[511,6,256]{2,1,0:T(8,128)} %copy.140), kind=kCustom, calls=%fused_computation.4.clone.clone.1 | custom fusion | flops 784896 | bytes 9420796 | tf_op jit(solution)/shard_map/while/body/eval_jaxpr/transpose(jvp(jit(_take)))/scatter-add | solution.py:37
  2701.0 11.5 pad_reduce_fusion.5
  2726.1 70.3 %scatter_fusion.1 = f32[6,256,512]{1,0,2:T(8,128)} fusion(f32[6,256,512]{1,0,2:T(8,128)} %broadcast.448, s32[511]{0:T(512)S(1)} %compare_select_fusion.7, f32[511,6,256]{2,1,0:T(8,128)} %copy.142), kind=kCustom, calls=%fused_computation.5.clone.clone.1 | custom fusion | flops 784896 | bytes 9420796 | tf_op jit(solution)/shard_map/while/body/eval_jaxpr/transpose(jvp(jit(_take)))/scatter-add | solution.py:39
  2860.3 17.9 reduce-scatter.3.cloned.1.call-done
  2880.3 264.8 %all-reduce.15.cloned.1.call-done = (f32[384,384]{0,1:T(8,128)}, f32[384,384]{0,1:T(8,128)}, f32[384,384]{0,1:T(8,128)}, f32[384,384]{1,0:T(8,128)}, f32[384,153...) async-done(((f32[384,384]{0,1:T(8,128)}, f32[384,384]{0,1:T(8,128)}, f32[384,384]{0,1:T(8,128)}, f32[384,384]{1,0:T(8,128)}, f32[384,1536]{1,0:T(8,128)}, ...) | async-done | bytes 7864336 | tf_op jit(solution)/shard_map/psum | solution.py:12
  3146.7 35.1 %all-reduce.8 = (f32[384]{0:T(512)S(1)}, f32[384]{0:T(512)S(1)}, f32[384]{0:T(512)S(1)}, f32[384]{0:T(512)S(1)}, f32[384]{0:T(512)S(1)}, /*index=5*/f32[384]{0:T...) all-reduce(f32[384]{0:T(512)S(1)} %add.549, ...), channel_id=1, replica_groups=mesh['blk'=4,'dp'=8] {'dp'}, use_global_device_ids=true, to_apply=%region_21.25 | all-reduce | flops 4992 | bytes 39936 | tf_op jit(solution)/shard_map/psum | solution.py:12
  3181.8 12.9 all-reduce.10
  3196.2 97.4 %all-reduce.17.cloned.1.call-done = (f32[384,384]{0,1:T(8,128)}, f32[384,384]{0,1:T(8,128)}, f32[384,384]{0,1:T(8,128)}, f32[384,384]{1,0:T(8,128)}, f32[384,153...) async-done(((f32[384,384]{0,1:T(8,128)}, f32[384,384]{0,1:T(8,128)}, f32[384,384]{0,1:T(8,128)}, f32[384,384]{1,0:T(8,128)}, f32[384,1536]{1,0:T(8,128)}, ...) | async-done | bytes 7864336 | tf_op jit(solution)/shard_map/psum | solution.py:13
  (561 shorter events, 719.3 us)
Async XLA Ops:
  7.2 1432.3 %copy-start = (bf16[384,1536]{1,0:T(8,128)(2,1)S(1)}, bf16[384,1536]{1,0:T(8,128)(2,1)}, u32[]{:S(2)}) copy-start(bf16[384,1536]{1,0:T(8,128)(2,1)} %param.40) | copy-start | bytes 3538948
  7.2 5.7 copy-start.15
  7.2 5.3 copy-start.20
  7.2 5.3 copy-start.22
  7.2 2851.1 %reduce-scatter.5.cloned.1.call-start = ((), (), s32[]{:S(2)}) async-start(), calls=%async_computation.3 | async-start | bytes 983040 | tf_op jit(solution)/shard_map/reduce_scatter | solution.py:248
  10.2 4.9 copy-start.81
  10.2 5.5 copy-start.79
  10.2 6.1 copy-start.82
  10.2 6.7 copy-start.83
  10.2 6.7 copy-start.42
  13.0 27.6 copy-start.6
  40.5 6.4 copy-start.18
  1261.8 7.1 copy-start.48
  1261.8 7.3 copy-start.25
  1269.7 4.0 copy-start.11
  1269.7 4.0 copy-start.58
  1273.7 10.2 copy-start.67
  1412.9 16.5 copy-start.19
  1437.4 7.5 copy-start.68
  1437.4 19.9 copy-start.59
  1438.8 6.1 copy-start.51
  1439.3 18.1 copy-start.13
  1439.3 18.1 copy-start.61
  1439.5 17.9 copy-start.63
  1439.5 5.4 copy-start.80
  1439.5 5.4 copy-start.88
  1446.9 7.6 copy-start.90
  1446.9 7.6 copy-start.91
  1457.7 5.1 copy-start.28
  1457.7 5.1 copy-start.65
  1458.4 4.4 copy-start.37
  1460.5 2.3 copy-start.7
  1460.5 2.3 copy-start.57
  1463.2 7.5 copy-start.8
  1567.0 2.7 copy-start.3
  1607.5 62.9 %copy-start.5 = (f32[1,6,256,256]{3,2,1,0:T(8,128)S(1)}, f32[1,6,256,256]{3,2,1,0:T(8,128)}, u32[]{:S(2)}) copy-start(f32[1,6,256,256]{3,2,1,0:T(8,128)} %get-tuple-element.743) | copy-start | bytes 4718596 | tf_op jit(solution)/shard_map/while
  1784.5 3.0 copy-start.4
  1792.7 7.5 copy-start.8
  1896.4 2.7 copy-start.3
  1937.9 66.6 %copy-start.5 = (f32[1,6,256,256]{3,2,1,0:T(8,128)S(1)}, f32[1,6,256,256]{3,2,1,0:T(8,128)}, u32[]{:S(2)}) copy-start(f32[1,6,256,256]{3,2,1,0:T(8,128)} %get-tuple-element.743) | copy-start | bytes 4718596 | tf_op jit(solution)/shard_map/while
  2122.2 3.3 copy-start.4
  2130.6 7.5 copy-start.8
  2234.4 2.7 copy-start.3
  2275.9 70.0 %copy-start.5 = (f32[1,6,256,256]{3,2,1,0:T(8,128)S(1)}, f32[1,6,256,256]{3,2,1,0:T(8,128)}, u32[]{:S(2)}) copy-start(f32[1,6,256,256]{3,2,1,0:T(8,128)} %get-tuple-element.743) | copy-start | bytes 4718596 | tf_op jit(solution)/shard_map/while
  2467.2 3.3 copy-start.4
  2475.6 7.5 copy-start.8
  2579.4 2.7 copy-start.3
  2620.9 70.0 %copy-start.5 = (f32[1,6,256,256]{3,2,1,0:T(8,128)S(1)}, f32[1,6,256,256]{3,2,1,0:T(8,128)}, u32[]{:S(2)}) copy-start(f32[1,6,256,256]{3,2,1,0:T(8,128)} %get-tuple-element.743) | copy-start | bytes 4718596 | tf_op jit(solution)/shard_map/while
  2812.2 3.3 copy-start.4
  2827.6 50.6 %reduce-scatter.3.cloned.1.call-start = ((), (), s32[]{:S(2)}) async-start(), calls=%async_computation.2 | async-start | bytes 983040 | tf_op jit(solution)/shard_map/reduce_scatter | solution.py:245
  2828.4 316.7 %all-reduce.15.cloned.1.call-start = ((), (), s32[]{:S(2)}) async-start(), calls=%async_computation.4 | async-start | bytes 15728640 | tf_op jit(solution)/shard_map/psum | solution.py:12
  2834.6 3.0 copy-start.26
  2848.7 2.1 copy-start.35
  2854.2 2.1 copy-start.14
  2854.2 2.1 copy-start.31
  2880.3 413.3 %all-reduce.17.cloned.1.call-start = ((), (), s32[]{:S(2)}) async-start(), calls=%async_computation.5 | async-start | bytes 15728640 | tf_op jit(solution)/shard_map/psum | solution.py:13
  3145.2 49.9 %copy-start.29 = (f32[1,256,384]{2,1,0:T(8,128)S(1)}, f32[1,256,384]{2,1,0:T(8,128)}, u32[]{:S(2)}) copy-start(f32[1,256,384]{2,1,0:T(8,128)} %copy-done.28) | copy-start | bytes 1179652
  3145.2 49.9 %copy-start.43 = (bf16[384,384]{1,0:T(8,128)(2,1)S(1)}, bf16[384,384]{1,0:T(8,128)(2,1)}, u32[]{:S(2)}) copy-start(bf16[384,384]{1,0:T(8,128)(2,1)} %param.34) | copy-start | bytes 884740
  3145.2 49.9 %copy-start.66 = (f32[256]{0:T(256)S(1)}, f32[256]{0:T(256)}, u32[]{:S(2)}) copy-start(f32[256]{0:T(256)} %copy-done.65) | copy-start | bytes 3076
  3293.6 4.5 copy-start.55
  3293.6 5.5 copy-start.54
  3295.8 4.1 copy-start.33
  3299.9 2.5 copy-start.32
  3302.4 2.6 copy-start.1
  (54 other events, 80.9 us)
Sparse Core Ops, SparseCore 0:
  2827.7 24.4 reduce-scatter.4
  2854.9 23.2 reduce-scatter.2
  2885.4 259.6 all-reduce.14
  3147.8 145.7 all-reduce.16
